TPU v7x, 256 devices: a whole 4x4x8 slice. The times are simulated.
256 devices in a mesh: prow: 16 (over z_hi, y), pcol: 16 (over z_lo, x, core).
Axes of the slice: x: 4, y: 4, z: 8 (z_hi: 4, z_lo: 2; z = z_hi * 2 + z_lo), core: 2. Of those that a mesh axis runs over, the one named last changes fastest.
Arguments:
- sigma_ancestors: float32 [16384, 16384], P('prow', 'pcol'), as said below
- panel_two: float32 [16384, 256], P('pcol'), may hold values from -0.0546875 to 0.0546875
- panel_one: float32 [16384, 256], P('pcol'), may hold values from -0.0625 to 0.0625
- panel_top: float32 [256, 256], replicated, may hold values from -0.375 to 0.375
- blocks_two: int32 [48], replicated, may hold values from 0 to 63, as said below
- blocks_one: int32 [32], replicated, may hold values from 0 to 63, as said below
- inverse_two: float32 [256, 256], replicated, as said below
- inverse_one: float32 [256, 256], replicated, as said below
Outputs:
- column_two: float32 [16384, 256], P('prow')
- diagonal_two: float32 [256, 256], replicated
- column_one: float32 [16384, 256], P('prow')
- coupling_one: float32 [256, 256], replicated
- diagonal_one: float32 [256, 256], replicated
Inputs may be any that keep to these rules, and one draw needn't show every extreme that they name: `blocks_two`: distinct and increasing; blocks 0, 32 and 63 are always listed. `blocks_one`: distinct and increasing, every one of them also listed in blocks_two; blocks 0, 32 and 63 are always listed. `sigma_ancestors`: symmetric positive definite. `inverse_two`: symmetric positive definite. `inverse_one`: symmetric positive definite.
All inputs are finite; a program needn't handle non-finite values.
Results may differ from a plain program's by a relative error of at most 0.000073.
Values sent between devices are 32-bit elements; how exact they have to be, the bound alone decides.
No kernel may reach another device: no remote copies, remote signals or barrier semaphores. Data moves between devices by JAX's collectives and lax.ppermute only.
A program may use at most 64 MiB of HBM per device.

v0:
```python
import jax
import jax.numpy as jnp
from jax import lax
from jax.sharding import PartitionSpec as P


def product(left, right):
    return jnp.dot(left, right, precision=lax.Precision.HIGHEST, preferred_element_type=jnp.float32)


def inner(left, right):
    return lax.dot_general(
        left,
        right,
        (((0,), (0,)), ((), ())),
        precision=lax.Precision.HIGHEST,
        preferred_element_type=jnp.float32,
    )


def block_mask(first_block, count, listed, block_width):
    block_ids = first_block + jnp.arange(count, dtype=jnp.int32)
    flags = jnp.any(block_ids[:, None] == listed[None, :], axis=1).astype(jnp.float32)
    return jnp.repeat(flags, block_width)[:, None]


def to_columns(rows_part):
    groups = lax.axis_size("prow") // lax.axis_size("pcol")
    column_index = lax.axis_index("pcol")
    row_index = lax.axis_index("prow")
    holding = (row_index // groups == column_index).astype(jnp.float32)
    placed = rows_part * holding
    return lax.psum(placed, "prow")


def per_device(
    sigma_ancestors,
    panel_two,
    panel_one,
    panel_top,
    blocks_two,
    blocks_one,
    inverse_two,
    inverse_one,
):
    block_width = panel_two.shape[1]
    row_count = sigma_ancestors.shape[0]
    col_count = sigma_ancestors.shape[1]
    row_first = lax.axis_index("prow") * (row_count // block_width)
    col_first = lax.axis_index("pcol") * (col_count // block_width)
    rows_mask_two = block_mask(row_first, row_count // block_width, blocks_two, block_width)
    rows_mask_one = block_mask(row_first, row_count // block_width, blocks_one, block_width)
    live_two = panel_two * block_mask(col_first, col_count // block_width, blocks_two, block_width)
    live_one = panel_one * block_mask(col_first, col_count // block_width, blocks_one, block_width)
    partial_two = product(sigma_ancestors, live_two)
    partial_one = product(sigma_ancestors, live_one)
    column_two = -rows_mask_two * lax.psum(partial_two, "pcol")
    column_two_cols = to_columns(column_two)
    cross_two = inner(live_two, column_two_cols)
    cross_one = inner(column_two_cols, live_one)
    diagonal_two = inverse_two - lax.psum(cross_two, "pcol")
    rows_total, top_total = lax.psum((partial_one, cross_one), "pcol")
    coupling_one = -(product(diagonal_two, panel_top) + top_total)
    column_one = -rows_mask_one * (rows_total + product(column_two, panel_top))
    column_one_cols = to_columns(column_one)
    diagonal_one = (
        inverse_one
        - lax.psum(inner(live_one, column_one_cols), "pcol")
        - inner(panel_top, coupling_one)
    )
    return (column_two, diagonal_two, column_one, coupling_one, diagonal_one)


def solution(mesh):
    in_specs = (P("prow", "pcol"), P("pcol", None), P("pcol", None), P(), P(), P(), P(), P())
    out_specs = (P("prow", None), P(), P("prow", None), P(), P())
    return jax.shard_map(
        per_device, mesh=mesh, in_specs=in_specs, out_specs=out_specs, check_vma=False
    )
```

profile of v0, /device:TPU:1, one launch (start us, length us, event | category | flops | bytes accessed | tf_op | source)
XLA Modules:
  0.0 489.8 jit_solution(4739473964338279017)
XLA Ops:
  7.2 0.0 copy-start
  7.2 0.0 copy-start.2
  7.2 0.0 all-reduce.9.cloned.1.call-start
  7.2 0.0 copy-start.1
  7.3 1.0 compare_reduce_fusion.1
  8.3 1.4 compare_reduce_fusion.3
  9.7 0.1 broadcast_bitcast_fusion
  9.8 0.1 broadcast_bitcast_fusion.2
  9.8 10.5 %convolution_bitcast_fusion.1 = f32[1024,256]{0,1:T(8,128)} fusion(f32[1024,1024]{1,0:T(8,128)} %param.8, f32[1024,256]{1,0:T(8,128)} %param.9, f32[1024]{0:T(1024)S(1)} %bitcast.34), kind=kOutput, calls=%fused_computation.1 | convolution fusion | flops 3221487616 | bytes 6295552 | tf_op jit(solution)/shard_map/dot_general | solution.py:8
  20.3 0.0 copy-done.2
  20.3 0.0 copy-done.1
  20.3 8.2 %convolution_bitcast_fusion = f32[1024,256]{0,1:T(8,128)} fusion(f32[1024,1024]{1,0:T(8,128)S(1)} %copy-done.1, f32[1024,256]{1,0:T(8,128)S(1)} %copy-done.2, f32[1024]{0:T(1024)S(1)} %bitcast.31), kind=kOutput, calls=%fused_computation | convolution fusion | flops 3221487616 | bytes 6295552 | tf_op jit(solution)/shard_map/dot_general | solution.py:8
  28.5 0.0 all-reduce.9.cloned.1.call-update
  28.6 0.0 all-reduce.11.cloned.1.call-start
  28.6 0.1 broadcast_bitcast_fusion.3
  28.7 0.1 broadcast_bitcast_fusion.1
  28.8 131.2 %all-reduce.9.cloned.1.call-done = (f32[1024,256]{0,1:T(8,128)}, f32[1024,256]{0,1:T(8,128)}) async-done(((f32[1024,256]{0,1:T(8,128)}, f32[1024,256]{0,1:T(8,128)}), (f32[1024,256]{0,1:T(8,128)}, f32[1024,256]{0,1:T(8,128)})) %all-reduce.9.cloned.1.call-update) | async-done | bytes 2097168 | tf_op jit(solution)/shard_map/psum | solution.py:57
  160.0 2.5 broadcast_multiply_fusion.1
  162.5 0.0 copy-done
  162.5 0.0 copy-start.3
  162.5 3.8 broadcast_multiply_fusion
  166.3 0.0 all-reduce.11.cloned.1.call-update
  166.3 0.0 all-reduce.7.cloned.1.call-start
  166.4 173.3 %all-reduce.11.cloned.1.call-done = (f32[1024,256]{0,1:T(8,128)}, f32[1024,256]{0,1:T(8,128)}) async-done(((f32[1024,256]{0,1:T(8,128)}, f32[1024,256]{0,1:T(8,128)}), (f32[1024,256]{0,1:T(8,128)}, f32[1024,256]{0,1:T(8,128)})) %all-reduce.11.cloned.1.call-update) | async-done | bytes 2097168 | tf_op jit(solution)/shard_map/psum | solution.py:33
  339.7 0.0 copy-start.5
  339.7 3.1 fusion.8
  342.8 0.0 copy-done.3
  342.8 3.9 fusion.3
  346.8 0.0 copy-start.4
  346.8 0.0 copy-done.5
  346.8 2.7 fusion.6
  349.5 0.0 copy-start.8
  349.5 0.0 all-reduce.7.cloned.1.call-update
  349.5 1.3 copy.19
  350.8 0.0 copy-done.4
  350.8 1.3 copy.20
  352.1 126.2 %all-reduce.7.cloned.1.call-done = (f32[256,256]{1,0:T(8,128)}, f32[256,256]{1,0:T(8,128)}, f32[256,256]{1,0:T(8,128)}) async-done(((f32[256,256]{1,0:T(8,128)}, f32[256,256]{1,0:T(8,128)}, f32[256,256]{1,0:T(8,128)}), (f32[256,256]{1,0:T(8,128)}, f32[256,256]{1,0:T(8,128)}, f32[256,256]{1,0:T(8,128)})) %all-reduce.7.cloned.1.call-update) | async-done | bytes 786448 | tf_op jit(solution)/shard_map/psum | solution.py:61
  478.3 1.1 sub.12
  479.4 0.0 copy-start.6
  479.4 1.4 fusion.2
  480.9 0.0 copy-start.7
  480.9 0.0 copy-done.8
  480.9 2.3 fusion.1
  483.2 0.0 copy-done.6
  483.2 0.0 copy-done.7
  (9 shorter events, 0.1 us)
Async XLA Ops:
  7.2 155.3 %copy-start = (f32[256,256]{1,0:T(8,128)S(1)}, f32[256,256]{1,0:T(8,128)}, u32[]{:S(2)}) copy-start(f32[256,256]{1,0:T(8,128)} %param.11) | copy-start | bytes 786436
  7.2 13.1 %copy-start.2 = (f32[1024,256]{1,0:T(8,128)S(1)}, f32[1024,256]{1,0:T(8,128)}, u32[]{:S(2)}) copy-start(f32[1024,256]{1,0:T(8,128)} %param.10) | copy-start | bytes 3145732
  7.2 152.8 %all-reduce.9.cloned.1.call-start = ((), (), s32[]{:S(2)}) async-start(), calls=%async_computation.1 | async-start | bytes 4194304 | tf_op jit(solution)/shard_map/psum | solution.py:57
  7.2 13.1 %copy-start.1 = (f32[1024,1024]{1,0:T(8,128)S(1)}, f32[1024,1024]{1,0:T(8,128)}, u32[]{:S(2)}) copy-start(f32[1024,1024]{1,0:T(8,128)} %param.8) | copy-start | bytes 12582916
  28.6 311.1 %all-reduce.11.cloned.1.call-start = ((), (), s32[]{:S(2)}) async-start(), calls=%async_computation.2 | async-start | bytes 4194304 | tf_op jit(solution)/shard_map/psum | solution.py:33
  162.5 180.4 %copy-start.3 = (f32[1024,256]{1,0:T(8,128)S(1)}, f32[1024,256]{1,0:T(8,128)}, u32[]{:S(2)}) copy-start(f32[1024,256]{1,0:T(8,128)} %param.9) | copy-start | bytes 3145732
  166.3 312.0 %all-reduce.7.cloned.1.call-start = ((), (), s32[]{:S(2)}) async-start(), calls=%async_computation | async-start | bytes 1572864 | tf_op jit(solution)/shard_map/psum | solution.py:61
  339.7 7.1 %copy-start.5 = (f32[1024,256]{0,1:T(8,128)S(1)}, f32[1024,256]{0,1:T(8,128)}, u32[]{:S(2)}) copy-start(f32[1024,256]{0,1:T(8,128)} %get-tuple-element.25) | copy-start | bytes 3145732
  346.8 4.0 copy-start.4
  349.5 131.4 %copy-start.8 = (f32[256,256]{1,0:T(8,128)S(1)}, f32[256,256]{1,0:T(8,128)}, u32[]{:S(2)}) copy-start(f32[256,256]{1,0:T(8,128)} %param.15) | copy-start | bytes 786436
  479.4 3.8 copy-start.6
  480.9 2.4 copy-start.7
Sparse Core Ops, SparseCore 0:
  28.7 131.2 all-reduce.8
  166.4 173.2 all-reduce.10
  349.6 128.6 all-reduce.6
where the time goes:
time: 490 us
  waiting for transfers between devices  431 us (88%)
  matrix products  36 us (7%)
  between operations  13.9 us (3%)
  other arithmetic  5.94 us (1%)
    psum x1, waiting for transfers between devices, to_columns(): return lax.psum(placed, 'prow')  173 us
    psum x1, waiting for transfers between devices, per_device(): column_two = -rows_mask_two * lax.psum(partial_two, 'pcol')  131 us
    psum x1, waiting for transfers between devices, per_device(): diagonal_two = inverse_two - lax.psum(cross_two, 'pcol')  126 us
    dot_general x4, matrix products, product(): jnp.dot(left, right, precision=lax.Precision.HIGHEST, preferred_element_t...  23.9 us
    dot_general x4, matrix products, inner(): lax.dot_general(left, right, (((0,), (0,)), ((), ())), precision=lax.Prec...  12.1 us
  transfers between devices with their start and end apart: 3, of which 3 were waited for; matrix products, arithmetic and copies ran while one was open for 1% of the time, Pallas kernels for 0%

commit v1 on v0

v1 whole, which is shorter than its diff:
```python
import functools

import jax
import jax.numpy as jnp
from jax import lax
from jax.experimental import pallas as pl
from jax.experimental.pallas import tpu as pltpu
from jax.sharding import Mesh, PartitionSpec as P

F32 = jnp.float32
BF16 = jnp.bfloat16
VMEM_LIMIT = 40 * 1024 * 1024
AXES = ("zh", "y", "zl", "x", "c")
SIZES = (4, 4, 2, 4, 2)
B = 256
CH = 64
ROWS = 1024


def split(value):
    high = value.astype(BF16)
    return high, (value - high.astype(F32)).astype(BF16)


def dot3(left, right, dims):
    lh, ll = left
    rh, rl = right
    go = functools.partial(lax.dot_general, dimension_numbers=(dims, ((), ())), preferred_element_type=F32)
    return go(lh, rh) + (go(lh, rl) + go(ll, rh))


MM = ((1,), (0,))
TM = ((0,), (0,))


def flag(listed, block):
    return jnp.max(jnp.where(listed == block, 1.0, 0.0), axis=1, keepdims=True)


def send_kernel(col_ref, s_ref, two_ref, one_ref, top_ref, b2_ref, b1_ref, p_ref, zh_ref, zl_ref):
    @pl.when(pl.program_id(0) == 0)
    def _():
        top = split(top_ref[...])
        first = col_ref[0] * (ROWS // B)
        for k in range(ROWS // B):
            rows = pl.ds(k * B, B)
            live_two = two_ref[rows, :] * flag(b2_ref[...], first + k)
            live_one = one_ref[rows, :] * flag(b1_ref[...], first + k)
            h2, l2 = split(live_two)
            hw, lw = split(live_one - dot3((h2, l2), top, MM))
            zh_ref[rows, :B] = h2
            zl_ref[rows, :B] = l2
            zh_ref[rows, B:] = hw
            zl_ref[rows, B:] = lw

    product_body(s_ref, zh_ref, zl_ref, p_ref)


def product_body(s_ref, zh_ref, zl_ref, p_ref):
    rows = s_ref.shape[0] * s_ref.shape[1]
    sigma = split(s_ref[...].reshape(rows, ROWS))
    p_ref[...] = dot3(sigma, (zh_ref[...], zl_ref[...]), MM)


def keep_kernel(col_ref, s_ref, zh_ref, zl_ref, p_ref):
    product_body(s_ref, zh_ref, zl_ref, p_ref)


def products(where, sigma, two, one, top, b2, b1):
    steps = 2
    per = 8 // steps
    sig = sigma.reshape(8, 2 * CH, ROWS)
    params = pltpu.CompilerParams(dimension_semantics=("arbitrary",), vmem_limit_bytes=VMEM_LIMIT)
    whole = lambda shape: pl.BlockSpec(shape, lambda i, w: (0,) * len(shape))
    out_p = pl.BlockSpec((per * CH, 2 * B), lambda i, w: (i, 0))
    send, zh, zl = pl.pallas_call(
        send_kernel,
        grid_spec=pltpu.PrefetchScalarGridSpec(
            num_scalar_prefetch=1,
            grid=(steps,),
            in_specs=[
                pl.BlockSpec((per, CH, ROWS), lambda i, w: (i, 1 - w[1], 0)),
                whole((ROWS, B)),
                whole((ROWS, B)),
                whole((B, B)),
                whole(b2.shape),
                whole(b1.shape),
            ],
            out_specs=[out_p, whole((ROWS, 2 * B)), whole((ROWS, 2 * B))],
        ),
        out_shape=[
            jax.ShapeDtypeStruct((8 * CH, 2 * B), F32),
            jax.ShapeDtypeStruct((ROWS, 2 * B), BF16),
            jax.ShapeDtypeStruct((ROWS, 2 * B), BF16),
        ],
        compiler_params=params,
        name="product_send",
    )(where, sig, two, one, top, b2, b1)

    got = lax.ppermute(send, "c", [(0, 1), (1, 0)])
    keep = pl.pallas_call(
        keep_kernel,
        grid_spec=pltpu.PrefetchScalarGridSpec(
            num_scalar_prefetch=1,
            grid=(steps,),
            in_specs=[
                pl.BlockSpec((per, CH, ROWS), lambda i, w: (i, w[1], 0)),
                whole((ROWS, 2 * B)),
                whole((ROWS, 2 * B)),
            ],
            out_specs=out_p,
        ),
        out_shape=jax.ShapeDtypeStruct((8 * CH, 2 * B), F32),
        compiler_params=params,
        cost_estimate=pl.CostEstimate(flops=3 * 2 * 512 * 1024 * 512, bytes_accessed=5 << 20, transcendentals=0),
        name="product_keep",
    )(where, sig, zh, zl)
    return keep + got


def gram_kernel(w_ref, y_ref, z_ref, top_ref, b2_ref, b1_ref, c2_ref, c1_ref, keep_ref, send_ref, g_ref):
    y = y_ref[pl.ds(0, CH), :]
    for k in range(1, 8):
        y = y + y_ref[pl.ds(k * CH, CH), :]
    block = w_ref[2]
    f2 = flag(b2_ref[...], block)
    f1 = flag(b1_ref[...], block)
    y2 = y[:, :B] * f2
    yw = y[:, B:]
    c2_ref[...] = -y2
    c1_ref[...] = -(yw * f1)
    live_two = split(z_ref[:, :B] * f2)
    w = split(z_ref[:, B:] * f1 - dot3(live_two, split(top_ref[...]), MM))
    yw = split(yw)
    g_ref[pl.ds(0, B), :] = dot3(live_two, split(y2), TM)
    g_ref[pl.ds(B, B), :] = dot3(live_two, yw, TM)
    g_ref[pl.ds(2 * B, B), :] = dot3(w, yw, TM)
    half = 3 * B // 2
    mine = w_ref[1]
    keep_ref[...] = g_ref[pl.ds(pl.multiple_of(mine * half, half), half), :]
    send_ref[...] = g_ref[pl.ds(pl.multiple_of((1 - mine) * half, half), half), :]


def gram(where, y, z, top, b2, b1):
    vm = pl.BlockSpec(memory_space=pltpu.VMEM)
    half = 3 * B // 2
    return pl.pallas_call(
        gram_kernel,
        in_specs=[pl.BlockSpec(memory_space=pltpu.SMEM)] + [vm] * 5,
        out_specs=[vm] * 4,
        out_shape=[
            jax.ShapeDtypeStruct((CH, B), F32),
            jax.ShapeDtypeStruct((CH, B), F32),
            jax.ShapeDtypeStruct((half, B), F32),
            jax.ShapeDtypeStruct((half, B), F32),
        ],
        scratch_shapes=[pltpu.VMEM((3 * B, B), F32)],
        compiler_params=pltpu.CompilerParams(vmem_limit_bytes=VMEM_LIMIT),
        name="gram",
    )(where, y, z, top, b2, b1)


def tops_kernel(top_ref, inv2_ref, inv1_ref, coup_ref, diag_ref):
    top = split(top_ref[...])
    it = dot3(split(inv2_ref[...]), top, MM)
    coup_ref[...] = it
    diag_ref[...] = inv1_ref[...] + dot3(top, split(it), TM)


def last_kernel(w_ref, mine_ref, other_ref, inv2_ref, it_ref, base_ref, d2_ref, cp_ref, d1_ref):
    half = 3 * B // 2

    def write(low, high):
        d2_ref[...] = inv2_ref[...] + low[pl.ds(0, B), :]
        cp_ref[pl.ds(0, B // 2), :] = low[pl.ds(B, B // 2), :] - it_ref[pl.ds(0, B // 2), :]
        cp_ref[pl.ds(B // 2, B // 2), :] = high[pl.ds(0, B // 2), :] - it_ref[pl.ds(B // 2, B // 2), :]
        d1_ref[...] = base_ref[...] + high[pl.ds(B // 2, B), :]

    @pl.when(w_ref[1] == 0)
    def _():
        write(mine_ref, other_ref)

    @pl.when(w_ref[1] == 1)
    def _():
        write(other_ref, mine_ref)


def a2a(value, axes):
    return lax.all_to_all(value, axes, 0, 0, tiled=True)


def per_device(sigma, two, one, top, blocks_two, blocks_one, inv2, inv1):
    zh, y, zl, x, c = (lax.axis_index(a) for a in AXES)
    row = zh * 4 + y
    col = zl * 8 + x * 2 + c
    where = jnp.stack([col, c, row * 4 + col // 4]).astype(jnp.int32)
    b2 = blocks_two.reshape(1, -1)
    b1 = blocks_one.reshape(1, -1)

    turn = [(i * 16 + j, j * 16 + i) for i in range(16) for j in range(16)]
    part = jnp.concatenate(
        [lax.dynamic_slice(p, (row * CH, 0), (CH, B)) for p in (two, one)], axis=1
    )
    z_rows = lax.ppermute(part, AXES, turn)

    pair = products(where, sigma, two, one, top, b2, b1)
    y_parts = a2a(pair, ("zl", "x"))
    c2, c1, keep, send = gram(where, y_parts, z_rows, top, b2, b1)
    column_two = lax.all_gather(c2, ("zl", "x", "c"), axis=0, tiled=True)
    column_one = lax.all_gather(c1, ("zl", "x", "c"), axis=0, tiled=True)

    vm = pl.BlockSpec(memory_space=pltpu.VMEM)
    square = jax.ShapeDtypeStruct((B, B), F32)
    it, base = pl.pallas_call(
        tops_kernel, in_specs=[vm] * 3, out_specs=[vm] * 2, out_shape=[square] * 2, name="tops"
    )(top, inv2, inv1)

    g = keep + lax.ppermute(send, "c", [(0, 1), (1, 0)])
    g = jnp.sum(a2a(g, ("y", "x")).reshape(16, 24, B), axis=0)
    g = jnp.broadcast_to(g[None], (8, 24, B)).reshape(8 * 24, B)
    g = jnp.sum(a2a(g, ("zh", "zl")).reshape(8, 24, B), axis=0)
    g = jnp.broadcast_to(g[None], (16, 24, B)).reshape(16 * 24, B)
    g = a2a(g, ("y", "x"))
    other = lax.ppermute(g, "c", [(0, 1), (1, 0)])
    d2, cp, d1 = pl.pallas_call(
        last_kernel,
        in_specs=[pl.BlockSpec(memory_space=pltpu.SMEM)] + [vm] * 5,
        out_specs=[vm] * 3,
        out_shape=[square] * 3,
        name="last",
    )(where, g, other, inv2, it, base)
    return column_two, d2, column_one, cp, d1


def solution(mesh):
    fine = Mesh(mesh.devices.reshape(SIZES), AXES)
    prow = ("zh", "y")
    pcol = ("zl", "x", "c")
    in_specs = (P(prow, pcol), P(pcol, None), P(pcol, None), P(), P(), P(), P(), P())
    out_specs = (P(prow, None), P(), P(prow, None), P(), P())
    return jax.shard_map(
        per_device, mesh=fine, in_specs=in_specs, out_specs=out_specs, check_vma=False
    )
```

time: 490 us -> 137 us (0.28)
  waiting for transfers between devices: 431 us -> 32.6 us
  blocking collectives: 0 us -> 48.6 us
  matrix products: 36 us -> 0 us
  starting transfers between devices: 0.12 us -> 14.2 us
  Pallas kernels: 0 us -> 12.6 us
  local copies, waits for them, and re-layouts: 2.97 us -> 13.1 us
    psum x3 -> x0, waiting for transfers between devices: 431 us -> none  [the longest x1 173 us: to_columns(): return lax.psum(placed, 'prow')]
    all_to_all x0 -> x3, blocking collectives: none -> 48.6 us  [a2a(): return lax.all_to_all(value, axes, 0, 0, tiled=True)]
    dot_general x8 -> x0, matrix products: 36 us -> none  [the longest x4 23.9 us: product(): jnp.dot(left, right, precision=lax.Precision.HIGHEST, preferred_element_t...]
    all_gather x0 -> x2, waiting for transfers between devices: none -> 18.5 us  [the longest x1 18.5 us: per_device(): column_one = lax.all_gather(c1, ('zl', 'x', 'c'), axis=0, tiled=True)]
    pallas_call x0 -> x5, Pallas kernels: none -> 12.6 us  [the longest x1 3.5 us: products(): pl.pallas_call(send_kernel, grid_spec=pltpu.PrefetchScalarGridSpec(num_sc...]
    ppermute x0 -> x4, starting transfers between devices: none -> 10.5 us  [the longest x1 3.38 us: per_device(): z_rows = lax.ppermute(part, AXES, turn)]
    unnamed x28 -> x26, local copies, waits for them, and re-layouts: 2.97 us -> 12.2 us
    all_to_all x0 -> x1, waiting for transfers between devices: none -> 8.8 us  [a2a(): return lax.all_to_all(value, axes, 0, 0, tiled=True)]
  transfers between devices with their start and end apart: 3 -> 7, of which waited for: 3 -> 4; matrix products, arithmetic and copies ran while one was open for 1% -> 1% of each run, Pallas kernels for 0% -> 6%
where the time goes in v1:
time: 137 us
  blocking collectives  48.6 us (35%)
  waiting for transfers between devices  32.6 us (24%)
  starting transfers between devices  14.2 us (10%)
  between operations  14.2 us (10%)
  local copies, waits for them, and re-layouts  13.1 us (10%)
  Pallas kernels  12.6 us (9%)
    all_to_all x3, blocking collectives, a2a(): return lax.all_to_all(value, axes, 0, 0, tiled=True)  48.6 us
    all_gather x1, waiting for transfers between devices, per_device(): column_one = lax.all_gather(c1, ('zl', 'x', 'c'), axis=0, tiled=True)  18.5 us
    unnamed x26, local copies, waits for them, and re-layouts  12.2 us
    all_to_all x1, waiting for transfers between devices, a2a(): return lax.all_to_all(value, axes, 0, 0, tiled=True)  8.8 us
    all_to_all x1, starting transfers between devices, a2a(): return lax.all_to_all(value, axes, 0, 0, tiled=True)  3.64 us
    pallas_call x1, Pallas kernels, products(): pl.pallas_call(send_kernel, grid_spec=pltpu.PrefetchScalarGridSpec(num_sc...  3.5 us
    ppermute x1, starting transfers between devices, per_device(): z_rows = lax.ppermute(part, AXES, turn)  3.38 us
    ppermute x1, starting transfers between devices, products(): got = lax.ppermute(send, 'c', [(0, 1), (1, 0)])  3.32 us
  transfers between devices with their start and end apart: 7, of which 4 were waited for; matrix products, arithmetic and copies ran while one was open for 1% of the time, Pallas kernels for 6%

profile of v1, /device:TPU:1, one launch (start us, length us, event | category | flops | bytes accessed | tf_op | source)
XLA Modules:
  0.0 136.7 jit_solution(9789668530208847775)
XLA Ops:
  7.2 0.1 pad_add_fusion.col_ref.w_ref
  7.3 0.0 copy-start.5
  7.3 0.0 copy-start
  7.3 2.2 %copy-done = f32[1024,1024]{1,0:T(8,128)S(1)} copy-done((f32[1024,1024]{1,0:T(8,128)S(1)}, f32[1024,1024]{1,0:T(8,128)}, u32[]{:S(2)}) %copy-start) | copy-done | bytes 4194328
  9.5 0.0 copy-start.1
  9.5 0.9 copy-done.1
  10.4 0.0 copy-start.3
  10.4 1.2 copy-done.3
  11.6 0.0 copy-start.4
  11.6 1.2 copy-done.4
  12.9 0.0 copy-start.6
  12.9 0.7 copy-done.6
  13.5 0.0 copy-start.8
  13.5 0.7 copy-done.8
  14.2 3.5 %product_send.1 = (f32[512,512]{1,0:T(8,128)S(1)}, bf16[1024,512]{1,0:T(8,128)(2,1)S(1)}, bf16[1024,512]{1,0:T(8,128)(2,1)S(1)}) custom-call(s32[3]{0:T(128)S(1)} %pad_add_fusion.col_ref.w_ref, f32[8,128,1024]{2,1,0:T(8,128)S(1)} %bitcast.10, f32[1024,256]{1,0:T(8,128)S(1)} %copy-done.3, f32[1024,256]{1,0:T(8,128)S(1)} %copy-done.4, ...), custom_call_target="tpu_custom_call" | custom-call | tf_op jit(solution)/shard_map/product_send/pallas_call | solution.py:76
  17.7 3.3 %collective-permute-start = (f32[512,512]{1,0:T(8,128)S(1)}, f32[512,512]{1,0:T(8,128)S(1)}, u32[]{:S(2)}, u32[]{:S(2)}) collective-permute-start(f32[512,512]{1,0:T(8,128)S(1)} %get-tuple-element.19), channel_id=1, source_target_pairs={{0,1},{1,0},{2,3},{3,2},{4,5},{5,4},{6,7},{7,6},{8,9},{9,8},{10,11... | collective-permute-start | bytes 3145736 | tf_op jit(solution)/shard_map/ppermute | solution.py:100
  21.0 2.8 %product_keep.1 = f32[512,512]{1,0:T(8,128)S(1)} custom-call(s32[3]{0:T(128)S(1)} %pad_add_fusion.col_ref.w_ref, f32[8,128,1024]{2,1,0:T(8,128)S(1)} %bitcast.11, bf16[1024,512]{1,0:T(8,128)(2,1)S(1)} %get-tuple-element.17.zh_ref, bf16[1024,512]{1,0:T(8,128)(2,1)S(1)} %get-tuple-element.18.zl_ref), custom_call_target="tpu_custom_call" | custom-call | flops 1610612736 | bytes 5242880 | tf_op jit(solution)/shard_map/product_keep/pallas_call | solution.py:101
  23.8 0.0 copy-start.2
  23.8 0.0 copy-start.7
  23.8 0.0 copy-start.9
  23.8 0.0 collective-permute-done
  23.8 1.2 add.27
  25.0 3.6 %all-to-all-start = ((f32[8,64,512]{2,1,0:T(8,128)}), f32[8,64,512]{2,1,0:T(8,128)S(1)}, u32[]{:S(2)}, u32[]{:S(2)}) async-start(f32[8,64,512]{2,1,0:T(8,128)} %bitcast.6), calls=%async_computation | async-start | bytes 2097152 | tf_op jit(solution)/shard_map/all_to_all | solution.py:189
  28.7 0.0 all-gather.3.cloned.1.call-start
  28.7 0.9 constant_dynamic-slice_fusion
  29.6 3.4 %collective-permute-start.1 = (f32[64,512]{1,0:T(8,128)S(1)}, f32[64,512]{1,0:T(8,128)S(1)}, u32[]{:S(2)}, u32[]{:S(2)}) collective-permute-start(f32[64,512]{1,0:T(8,128)S(1)} %pad_maximum_fusion), channel_id=1, source_target_pairs={{0,0},{1,16},{2,32},{3,48},{4,64},{5,80},{6,96},{7,112},{8,128},{9... | collective-permute-start | bytes 393224 | tf_op jit(solution)/shard_map/ppermute | solution.py:204
  33.0 3.2 %collective-permute-done.1.z_ref = f32[64,512]{1,0:T(8,128)S(1)} collective-permute-done((f32[64,512]{1,0:T(8,128)S(1)}, f32[64,512]{1,0:T(8,128)S(1)}, u32[]{:S(2)}, u32[]{:S(2)}) %collective-permute-start.1) | collective-permute-done | bytes 131104 | tf_op jit(solution)/shard_map/ppermute | solution.py:204
  36.2 8.8 %all-to-all-done = f32[8,64,512]{2,1,0:T(8,128)S(1)} async-done(((f32[8,64,512]{2,1,0:T(8,128)}), f32[8,64,512]{2,1,0:T(8,128)S(1)}, u32[]{:S(2)}, u32[]{:S(2)}) %all-to-all-start) | async-done | bytes 1048608 | tf_op jit(solution)/shard_map/all_to_all | solution.py:189
  45.0 0.0 copy-done.5
  45.0 0.0 copy-done.2
  45.0 0.0 copy-done.7
  45.0 0.0 copy-done.9
  45.0 1.5 %gram.1 = (f32[64,256]{1,0:T(8,128)}, f32[64,256]{1,0:T(8,128)}, f32[384,256]{1,0:T(8,128)S(1)}, f32[384,256]{1,0:T(8,128)S(1)}) custom-call(s32[3]{0:T(128)S(1)} %pad_add_fusion.col_ref.w_ref, f32[512,512]{1,0:T(8,128)S(1)} %bitcast.12, f32[64,512]{1,0:T(8,128)S(1)} %collective-permute-done.1.z_ref, f32[256,256]{1,0:T(8,128)S(1)} %copy-done.2, ...), custom_call_target="tpu_custom_call" | custom-call | tf_op jit(solution)/shard_map/gram/pallas_call | solution.py:147
  46.5 0.0 all-gather.3.cloned.1.call-update
  46.5 0.0 all-gather.5.cloned.1.call-start
  46.6 0.7 all-gather.5.cloned.1.call-update
  47.3 1.2 collective-permute-start.2
  48.5 1.3 collective-permute-done.2
  49.8 0.1 add.29
  49.9 17.3 %all_to_all.34 = f32[16,24,256]{2,1,0:T(8,128)S(1)} all-to-all(f32[16,24,256]{2,1,0:T(8,128)S(1)} %bitcast.19), channel_id=1, replica_groups=mesh['zh'=4,'y'=4,'zl'=2,'x'=4,'c'=2] {'y','x'}, dimensions={0} | all-to-all | bytes 786432 | tf_op jit(solution)/shard_map/all_to_all | solution.py:189
  67.2 20.2 %all_to_all.35 = f32[8,24,256]{2,1,0:T(8,128)S(1)} all-to-all(f32[8,24,256]{2,1,0:T(8,128)S(1)} %broadcast_in_dim.4), channel_id=1, replica_groups=mesh['zh'=4,'y'=4,'zl'=2,'x'=4,'c'=2] {'zh','zl'}, dimensions={0} | all-to-all | bytes 393216 | tf_op jit(solution)/shard_map/all_to_all | solution.py:189
  87.4 11.2 %all_to_all.36 = f32[16,24,256]{2,1,0:T(8,128)S(1)} all-to-all(f32[16,24,256]{2,1,0:T(8,128)S(1)} %broadcast_in_dim.5), channel_id=1, replica_groups=mesh['zh'=4,'y'=4,'zl'=2,'x'=4,'c'=2] {'y','x'}, dimensions={0} | all-to-all | bytes 786432 | tf_op jit(solution)/shard_map/all_to_all | solution.py:189
  98.6 0.0 copy-start.10
  98.6 2.6 %collective-permute-start.3 = (f32[384,256]{1,0:T(8,128)S(1)}, f32[384,256]{1,0:T(8,128)S(1)}, u32[]{:S(2)}, u32[]{:S(2)}) collective-permute-start(f32[384,256]{1,0:T(8,128)S(1)} %bitcast.17), channel_id=1, source_target_pairs={{0,1},{1,0},{2,3},{3,2},{4,5},{5,4},{6,7},{7,6},{8,9},{9,8},{10,11... | collective-permute-start | bytes 1179656 | tf_op jit(solution)/shard_map/ppermute | solution.py:224
  101.3 2.5 %tops.1 = (f32[256,256]{1,0:T(8,128)}, f32[256,256]{1,0:T(8,128)}) custom-call(f32[256,256]{1,0:T(8,128)} %top_ref.5, f32[256,256]{1,0:T(8,128)} %inv2_ref.3, f32[256,256]{1,0:T(8,128)} %inv1_ref.1), custom_call_target="tpu_custom_call" | custom-call | tf_op jit(solution)/shard_map/tops/pallas_call | solution.py:214
  103.7 0.0 collective-permute-done.3.other_ref
  103.7 0.0 copy-start.11
  103.7 0.0 copy-done.10
  103.8 0.7 copy-done.11
  104.5 2.3 %last.1 = (f32[256,256]{1,0:T(8,128)}, f32[256,256]{1,0:T(8,128)}, f32[256,256]{1,0:T(8,128)}) custom-call(s32[3]{0:T(128)} %copy-done.5, f32[384,256]{1,0:T(8,128)} %bitcast.18, f32[384,256]{1,0:T(8,128)} %copy-done.11, f32[256,256]{1,0:T(8,128)} %inv2_ref.3, f32[256,256]{1,0:T(8,128)} %get-tuple-element.23.it_ref, f32[256,256]{1,0:T(8,128)} %get-tuple-element.24.base_ref), custom_call_target="tpu_custom_call" | custom-call | tf_op jit(solution)/shard_map/last/pallas_call | solution.py:225
  106.8 0.0 all-gather.3.cloned.1.call-done
  106.8 18.5 %all-gather.5.cloned.1.call-done = f32[1024,256]{1,0:T(8,128)} async-done(((f32[64,256]{1,0:T(8,128)}), f32[1024,256]{1,0:T(8,128)}) %all-gather.5.cloned.1.call-update) | async-done | bytes 1048592 | tf_op jit(solution)/shard_map/all_gather | solution.py:210
  125.3 2.3 %copy.15 = f32[1024,256]{1,0:T(8,128)} copy(f32[1024,256]{1,0:T(8,128)} %all-gather.3.cloned.1.call-done) | data formatting | bytes 2097152
  127.6 2.3 %copy.16 = f32[1024,256]{1,0:T(8,128)} copy(f32[1024,256]{1,0:T(8,128)} %all-gather.5.cloned.1.call-done) | data formatting | bytes 2097152
  (5 shorter events, 0.1 us)
Async XLA Ops:
  7.3 37.7 %copy-start.5 = (s32[3]{0:T(128)}, s32[3]{0:T(128)S(1)}, u32[]{:S(2)}) copy-start(s32[3]{0:T(128)S(1)} %pad_add_fusion.col_ref.w_ref) | copy-start | bytes 40
  7.3 2.2 %copy-start = (f32[1024,1024]{1,0:T(8,128)S(1)}, f32[1024,1024]{1,0:T(8,128)}, u32[]{:S(2)}) copy-start(f32[1024,1024]{1,0:T(8,128)} %param.8) | copy-start | bytes 12582916
  9.5 0.9 copy-start.1
  10.4 1.2 copy-start.3
  11.6 1.2 copy-start.4
  12.9 0.7 copy-start.6
  13.5 0.7 copy-start.8
  17.7 6.2 %collective-permute-start = (f32[512,512]{1,0:T(8,128)S(1)}, f32[512,512]{1,0:T(8,128)S(1)}, u32[]{:S(2)}, u32[]{:S(2)}) collective-permute-start(f32[512,512]{1,0:T(8,128)S(1)} %get-tuple-element.19), channel_id=1, source_target_pairs={{0,1},{1,0},{2,3},{3,2},{4,5},{5,4},{6,7},{7,6},{8,9},{9,8},{10,11... | collective-permute-start | bytes 3145736 | tf_op jit(solution)/shard_map/ppermute | solution.py:100
  23.8 21.2 %copy-start.2 = (f32[256,256]{1,0:T(8,128)S(1)}, f32[256,256]{1,0:T(8,128)}, u32[]{:S(2)}) copy-start(f32[256,256]{1,0:T(8,128)} %top_ref.5) | copy-start | bytes 786436
  23.8 21.2 %copy-start.7 = (s32[48]{0:T(128)S(1)}, s32[48]{0:T(128)}, u32[]{:S(2)}) copy-start(s32[48]{0:T(128)} %param.12) | copy-start | bytes 580
  23.8 21.2 %copy-start.9 = (s32[32]{0:T(128)S(1)}, s32[32]{0:T(128)}, u32[]{:S(2)}) copy-start(s32[32]{0:T(128)} %param.13) | copy-start | bytes 388
  25.0 20.0 %all-to-all-start = ((f32[8,64,512]{2,1,0:T(8,128)}), f32[8,64,512]{2,1,0:T(8,128)S(1)}, u32[]{:S(2)}, u32[]{:S(2)}) async-start(f32[8,64,512]{2,1,0:T(8,128)} %bitcast.6), calls=%async_computation | async-start | bytes 2097152 | tf_op jit(solution)/shard_map/all_to_all | solution.py:189
  28.7 78.2 %all-gather.3.cloned.1.call-start = ((), (), s32[]{:S(2)}) async-start(), calls=%async_computation.4 | async-start | bytes 1114112 | tf_op jit(solution)/shard_map/all_gather | solution.py:209
  29.6 6.6 %collective-permute-start.1 = (f32[64,512]{1,0:T(8,128)S(1)}, f32[64,512]{1,0:T(8,128)S(1)}, u32[]{:S(2)}, u32[]{:S(2)}) collective-permute-start(f32[64,512]{1,0:T(8,128)S(1)} %pad_maximum_fusion), channel_id=1, source_target_pairs={{0,0},{1,16},{2,32},{3,48},{4,64},{5,80},{6,96},{7,112},{8,128},{9... | collective-permute-start | bytes 393224 | tf_op jit(solution)/shard_map/ppermute | solution.py:204
  46.5 78.8 %all-gather.5.cloned.1.call-start = ((), (), s32[]{:S(2)}) async-start(), calls=%async_computation.5 | async-start | bytes 1114112 | tf_op jit(solution)/shard_map/all_gather | solution.py:210
  47.3 2.5 %collective-permute-start.2 = (f32[384,256]{1,0:T(8,128)S(1)}, f32[384,256]{1,0:T(8,128)S(1)}, u32[]{:S(2)}, u32[]{:S(2)}) collective-permute-start(f32[384,256]{1,0:T(8,128)S(1)} %get-tuple-element.22), channel_id=1, source_target_pairs={{0,1},{1,0},{2,3},{3,2},{4,5},{5,4},{6,7},{7,6},{8,9},{9,8},{10,11... | collective-permute-start | bytes 1179656 | tf_op jit(solution)/shard_map/ppermute | solution.py:218
  98.6 5.1 %copy-start.10 = (f32[16,24,256]{2,1,0:T(8,128)}, f32[16,24,256]{2,1,0:T(8,128)S(1)}, u32[]{:S(2)}) copy-start(f32[16,24,256]{2,1,0:T(8,128)S(1)} %all_to_all.36) | copy-start | bytes 1179652
  98.6 5.1 %collective-permute-start.3 = (f32[384,256]{1,0:T(8,128)S(1)}, f32[384,256]{1,0:T(8,128)S(1)}, u32[]{:S(2)}, u32[]{:S(2)}) collective-permute-start(f32[384,256]{1,0:T(8,128)S(1)} %bitcast.17), channel_id=1, source_target_pairs={{0,1},{1,0},{2,3},{3,2},{4,5},{5,4},{6,7},{7,6},{8,9},{9,8},{10,11... | collective-permute-start | bytes 1179656 | tf_op jit(solution)/shard_map/ppermute | solution.py:224
  103.7 0.7 copy-start.11
Sparse Core Ops, SparseCore 0:
  46.6 41.7 all-gather.2
  90.3 35.0 all-gather.4
